TPU v7x, 32 devices: a whole 2x2x4 slice. The times are simulated.
32 devices in a mesh: dp: 4 (over x, core), point: 8 (over z, y).
Axes of the slice: x: 2, y: 2, z: 4, core: 2. Of those that a mesh axis runs over, the one named last changes fastest.
Arguments:
- points: bfloat16 [262144, 256], P(('dp', 'point')), parts along dimension 0, may hold values from -6 to 6
- tree_order: int32 [262144], P(('dp', 'point')), parts along dimension 0, may hold values from 0 to 65535, as said below
- ball_counts: int32 [1024], P(('dp', 'point')), parts along dimension 0, may hold values from 64 to 256, as said below
- ball_proj: bfloat16 [3, 256, 256], replicated
- ball_out: bfloat16 [256, 256], replicated, may hold values from -0.375 to 0.375
- pool_weight: bfloat16 [16384, 256], replicated, may hold values from -0.046875 to 0.046875
- coarse_proj: bfloat16 [3, 256, 256], replicated
- coarse_out: bfloat16 [256, 256], replicated, may hold values from -6 to 6
- global_proj: bfloat16 [3, 256, 256], replicated
- global_out: bfloat16 [256, 256], replicated, may hold values from -6 to 6
- unpool_weight: bfloat16 [256, 16384], replicated, may hold values from -0.125 to 0.125
- mlp_in: bfloat16 [256, 1024], replicated, may hold values from -0.375 to 0.375
- mlp_out: bfloat16 [1024, 256], replicated, may hold values from -0.1875 to 0.1875
Outputs:
- result: bfloat16 [262144, 256], P(('dp', 'point')), parts along dimension 0
There are 4 independent parts, one for each index of `dp`. A program takes and returns all parts, laid end to end along the dimension named above; an argument that names none is the same for every part. Nothing has to cross between parts.
Inputs may be any that keep to these rules, and one draw needn't show every extreme that they name: `tree_order`: each block of 8192 slots takes a permutation of the same block of rows. `ball_counts`: live points come first in each ball; every block of 8192 slots holds a full ball.
All inputs are finite; a program needn't handle non-finite values.
Results may differ from a plain program's by a relative error of at most 0.03.
Values may be sent and summed in bfloat16 or wider, within the bound.
A program may use at most 256 MiB of HBM per device.

v0:
```python
import functools
import math

import jax
import jax.numpy as jnp
from jax import lax
from jax.experimental import pallas as pl
from jax.experimental.pallas import tpu as pltpu
from jax.sharding import PartitionSpec as P

HEADS = 8
BALL = 256
POOL = 64
EPSILON = 1e-05
F32 = jnp.float32
BF16 = jnp.bfloat16
MESH = pl.DeviceIdType.MESH
NT = (((1,), (1,)), ((), ()))
TN = (((0,), (0,)), ((), ()))


def normalize(inputs):
    center = inputs - jnp.mean(inputs, axis=-1, keepdims=True)
    spread = jnp.mean(center * center, axis=-1, keepdims=True)
    return (center * lax.rsqrt(spread + EPSILON)).astype(BF16)


def nt(a, b):
    return lax.dot_general(a, b, NT, preferred_element_type=F32)


def nn(a, b):
    return jnp.dot(a, b, preferred_element_type=F32)


def attend(q_in, kv_in, proj_ref, out_weight, valid):
    feature = q_in.shape[1]
    head = feature // HEADS
    rows, keys = q_in.shape[0], kv_in.shape[0]
    factor = math.log2(math.e) / math.sqrt(head)
    q_t = (nt(proj_ref[0], q_in) * factor).astype(BF16)
    k = nn(kv_in, proj_ref[1]).astype(BF16)
    v_t = nt(proj_ref[2], kv_in).astype(BF16)
    ones = jnp.ones((16, keys), BF16)
    outs = []
    for h in range(HEADS):
        lo, hi = h * head, (h + 1) * head
        parts = []
        if lo:
            parts.append(jnp.zeros((lo, rows), BF16))
        parts.append(q_t[lo:hi])
        if hi < feature:
            parts.append(jnp.zeros((feature - hi, rows), BF16))
        scores = nn(k, jnp.concatenate(parts, axis=0))
        if valid is not None:
            scores = jnp.where(valid, scores, -1e30)
        top = jnp.max(scores, axis=0, keepdims=True)
        expo = jnp.exp2(scores - top).astype(BF16)
        mixed = nn(jnp.concatenate([v_t[lo:hi], ones], axis=0), expo)
        outs.append((mixed[:head] * (1.0 / mixed[head : head + 1])).astype(BF16))
    return lax.dot_general(
        jnp.concatenate(outs, axis=0), out_weight, TN, preferred_element_type=F32
    )


def ball_kernel(
    order_ref, counts_ref, points_ref, proj_ref, out_ref, pool_ref,
    fine_ref, pooled_ref, wide, rows_ref, kept, pool_all,
):
    step = pl.program_id(0)
    steps = pl.num_programs(0)
    row_count = points_ref.shape[0]
    feature = points_ref.shape[1]
    pool_rows = pool_ref.shape[0]
    groups = row_count // POOL

    @pl.when(step == 0)
    def _():
        rows_ref[...] = jnp.zeros_like(rows_ref)

        def widen(t, carry):
            at = pl.ds(pl.multiple_of(t * BALL, BALL), BALL)
            wide[at, :] = points_ref[at, :].astype(F32)
            return carry

        lax.fori_loop(0, row_count // BALL, widen, 0)

    pool_all[pl.ds(pl.multiple_of(step * pool_rows, pool_rows), pool_rows), :] = pool_ref[...]
    count = counts_ref[step]
    first = step * BALL

    def take(g, carry):
        base = pl.multiple_of(g * 16, 16)
        for r in range(16):
            rows_ref[pl.ds(base + r, 1), :] = wide[pl.ds(order_ref[first + base + r], 1), :]
        return carry

    lax.fori_loop(0, (count + 15) // 16, take, 0)

    x = rows_ref[...]
    normed = normalize(x)
    valid = lax.broadcasted_iota(jnp.int32, (BALL, BALL), 0) < count
    fine = (x + attend(normed, normed, proj_ref, out_ref[...], valid)).astype(BF16)
    fine_ref[...] = fine
    live = lax.broadcasted_iota(jnp.int32, (BALL, feature), 0) < count
    at = pl.ds(pl.multiple_of(first, BALL), BALL)
    masked = jnp.where(live, fine.astype(F32), 0.0)
    for c in range(feature // 128):
        kept[c, at, :] = masked[:, c * 128 : (c + 1) * 128]

    @pl.when(step == steps - 1)
    def _():
        per = 8

        def pool(c, total):
            parts = []
            for r in range(per):
                for half in range(feature // 128):
                    parts.append(kept[half, pl.ds(c * per + r, groups, stride=POOL), :].astype(BF16))
            block = pl.ds(pl.multiple_of(c * (per * feature), per * feature), per * feature)
            return total + nn(jnp.concatenate(parts, axis=1), pool_all[block, :])

        total = lax.fori_loop(0, POOL // per, pool, jnp.zeros((groups, feature), F32))
        pooled_ref[...] = total.astype(BF16)


def ball_call(order, counts, points, proj, out_weight, pool_weight):
    row_count, feature = points.shape
    steps = row_count // BALL
    groups = row_count // POOL
    pool_rows = pool_weight.shape[0] // steps
    once = pl.Buffered(1)
    return pl.pallas_call(
        ball_kernel,
        grid_spec=pltpu.PrefetchScalarGridSpec(
            num_scalar_prefetch=2,
            grid=(steps,),
            in_specs=[
                pl.BlockSpec((row_count, feature), lambda i, *_: (0, 0), pipeline_mode=once),
                pl.BlockSpec(proj.shape, lambda i, *_: (0, 0, 0), pipeline_mode=once),
                pl.BlockSpec(out_weight.shape, lambda i, *_: (0, 0), pipeline_mode=once),
                pl.BlockSpec((pool_rows, feature), lambda i, *_: (i, 0)),
            ],
            out_specs=[
                pl.BlockSpec((BALL, feature), lambda i, *_: (i, 0)),
                pl.BlockSpec((groups, feature), lambda i, *_: (0, 0)),
            ],
            scratch_shapes=[
                pltpu.VMEM((row_count, feature), F32),
                pltpu.VMEM((BALL, feature), F32),
                pltpu.VMEM((feature // 128, row_count, 128), F32),
                pltpu.VMEM(pool_weight.shape, BF16),
            ],
        ),
        out_shape=[
            jax.ShapeDtypeStruct((row_count, feature), BF16),
            jax.ShapeDtypeStruct((groups, feature), BF16),
        ],
        compiler_params=pltpu.CompilerParams(vmem_limit_bytes=48 * 1024 * 1024),
        name="balls",
    )(order, counts, points, proj, out_weight, pool_weight)


def coarse_kernel(
    n, pooled_ref, fine_ref, cproj_ref, cout_ref, gproj_ref, gout_ref, win_ref, wout_ref,
    summary_ref, refined_ref, arrived, state, send_sem, recv_sem,
):
    me = lax.axis_index("point")
    tokens, feature = pooled_ref.shape
    row_count = fine_ref.shape[0]

    barrier = pltpu.get_barrier_semaphore()

    def greet(k, carry):
        peer = (me + k) % n
        pl.semaphore_signal(barrier, inc=1, device_id={"point": peer}, device_id_type=MESH)
        return carry

    lax.fori_loop(1, n, greet, 0)
    pl.semaphore_wait(barrier, n - 1)

    def copy_to(peer, slot, sender):
        return pltpu.make_async_remote_copy(
            src_ref=pooled_ref,
            dst_ref=arrived.at[sender],
            send_sem=send_sem.at[slot],
            recv_sem=recv_sem.at[sender],
            device_id={"point": peer},
            device_id_type=MESH,
        )

    def send(k, carry):
        copy_to((me + k) % n, k, me).start()
        return carry

    lax.fori_loop(1, n, send, 0)

    tile = 256

    def mlp(t, carry):
        at = pl.ds(pl.multiple_of(t * tile, tile), tile)
        fine = fine_ref[at, :].astype(F32)
        hidden = nn(normalize(fine), win_ref[...])
        expanded = jax.nn.gelu(hidden, approximate=True).astype(BF16)
        refined_ref[at, :] = (fine + nn(expanded, wout_ref[...])).astype(BF16)
        return carry

    lax.fori_loop(0, row_count // tile, mlp, 0)

    def land(k, carry):
        sender = (me + k) % n
        copy_to(sender, k, sender).wait_recv()
        state[pl.ds(pl.multiple_of(sender * tokens, tokens), tokens), :] = arrived[sender].astype(F32)
        return carry

    lax.fori_loop(1, n, land, 0)
    mine = pl.ds(pl.multiple_of(me * tokens, tokens), tokens)
    state[mine, :] = pooled_ref[...].astype(F32)

    apart = 1
    while apart < n:

        def pair(p, carry, apart=apart):
            low = (p // apart) * (2 * apart) + p % apart
            one = pl.ds(pl.multiple_of(low * tokens, tokens), tokens)
            two = pl.ds(pl.multiple_of((low + apart) * tokens, tokens), tokens)
            x = jnp.concatenate([state[one, :], state[two, :]], axis=0)
            normed = normalize(x)
            x = x + attend(normed, normed, cproj_ref, cout_ref[...], None)
            state[one, :] = x[:tokens]
            state[two, :] = x[tokens:]
            return carry

        lax.fori_loop(0, n // 2, pair, 0)
        apart *= 2

    x = state[mine, :]
    mixed = attend(normalize(x), normalize(state[...]), gproj_ref, gout_ref[...], None)
    summary_ref[...] = (x + mixed).astype(BF16)

    def sent(k, carry):
        copy_to((me + k) % n, k, me).wait_send()
        return carry

    lax.fori_loop(1, n, sent, 0)


def coarse_call(n, pooled, fine, cproj, cout, gproj, gout, mlp_in, mlp_out):
    tokens, feature = pooled.shape
    vmem = pl.BlockSpec(memory_space=pltpu.VMEM)
    return pl.pallas_call(
        functools.partial(coarse_kernel, n),
        in_specs=[vmem] * 8,
        out_specs=[vmem] * 2,
        out_shape=[
            jax.ShapeDtypeStruct((tokens, feature), BF16),
            jax.ShapeDtypeStruct(fine.shape, BF16),
        ],
        scratch_shapes=[
            pltpu.VMEM((n, tokens, feature), BF16),
            pltpu.VMEM((n * tokens, feature), F32),
            pltpu.SemaphoreType.DMA((n,)),
            pltpu.SemaphoreType.DMA((n,)),
        ],
        compiler_params=pltpu.CompilerParams(
            collective_id=0, has_side_effects=True, vmem_limit_bytes=40 * 1024 * 1024
        ),
        name="coarse",
    )(pooled, fine, cproj, cout, gproj, gout, mlp_in, mlp_out)


def unpool_kernel(half, counts_ref, summary_ref, weight_ref, refined_ref, out_ref, spread):
    step = pl.program_id(0)
    tokens, feature = summary_ref.shape
    per = weight_ref.shape[1] // feature
    rows = out_ref.shape[0]

    @pl.when(step < half)
    def _():
        for r in range(per):
            piece = nn(summary_ref[...], weight_ref[:, r * feature : (r + 1) * feature])
            for c in range(feature // 128):
                spread[c, pl.ds(step * per + r, tokens, stride=POOL), :] = piece[:, c * 128 : (c + 1) * 128]

    @pl.when(step >= half)
    def _():
        at = step - half
        for b in range(rows // BALL):
            here = slice(b * BALL, (b + 1) * BALL)
            count = counts_ref[at * (rows // BALL) + b]
            live = lax.broadcasted_iota(jnp.int32, (BALL, feature), 0) < count
            slots = pl.ds(pl.multiple_of(at * rows + b * BALL, BALL), BALL)
            wide = jnp.concatenate([spread[c, slots, :] for c in range(feature // 128)], axis=1)
            total = refined_ref[here, :].astype(F32) + wide
            out_ref[here, :] = jnp.where(live, total, 0.0).astype(BF16)


def unpool_call(counts, summary, weight, refined):
    row_count, feature = refined.shape
    half = 8
    rows = row_count // half
    columns = weight.shape[1] // half
    return pl.pallas_call(
        functools.partial(unpool_kernel, half),
        grid_spec=pltpu.PrefetchScalarGridSpec(
            num_scalar_prefetch=1,
            grid=(2 * half,),
            in_specs=[
                pl.BlockSpec(summary.shape, lambda i, *_: (0, 0)),
                pl.BlockSpec((feature, columns), lambda i, *_: (0, jnp.minimum(i, half - 1))),
                pl.BlockSpec((rows, feature), lambda i, *_: (jnp.maximum(i - half, 0), 0)),
            ],
            out_specs=pl.BlockSpec((rows, feature), lambda i, *_: (jnp.maximum(i - half, 0), 0)),
            scratch_shapes=[pltpu.VMEM((feature // 128, row_count, 128), F32)],
        ),
        out_shape=jax.ShapeDtypeStruct((row_count, feature), BF16),
        compiler_params=pltpu.CompilerParams(vmem_limit_bytes=32 * 1024 * 1024),
        name="unpool",
    )(counts, summary, weight, refined)


def turned(proj):
    return jnp.stack([proj[0].T, proj[1], proj[2].T])


def local(
    points, tree_order, ball_counts, ball_proj, ball_out, pool_weight, coarse_proj, coarse_out,
    global_proj, global_out, unpool_weight, mlp_in, mlp_out,
):
    n = lax.axis_size("point")
    order = tree_order - lax.axis_index("point") * points.shape[0]
    fine, pooled = ball_call(order, ball_counts, points, turned(ball_proj), ball_out, pool_weight)
    summary, refined = coarse_call(
        n, pooled, fine, turned(coarse_proj), coarse_out, turned(global_proj), global_out, mlp_in, mlp_out
    )
    return unpool_call(ball_counts, summary, unpool_weight, refined)


def solution(mesh):
    rows = P(("dp", "point"), None)
    line = P(("dp", "point"))
    return jax.shard_map(
        local,
        mesh=mesh,
        in_specs=(rows, line, line) + (P(),) * 10,
        out_specs=rows,
        check_vma=False,
    )
```

profile of v0, /device:TPU:0, one launch (start us, length us, event | category | flops | bytes accessed | tf_op | source)
XLA Modules:
  0.0 217.5 jit_solution(16609241101975389614)
XLA Ops:
  0.0 0.8 broadcast_subtract_fusion.order_ref
  0.8 1.1 fusion.2
  1.9 0.1 copy.20
  2.0 0.1 copy.21
  2.1 1.1 fusion.1
  3.2 0.1 copy.22
  3.3 0.1 copy.23
  3.4 1.1 fusion
  4.5 0.1 copy.24
  4.6 0.1 copy.25
  4.7 0.1 pad_maximum_fusion.1
  4.8 0.0 slice-start
  4.8 0.0 copy-start.2
  4.8 0.0 copy-start.3
  4.8 0.0 copy-start.5
  4.8 0.0 copy-start.6
  4.9 0.0 slice-start.1
  4.9 123.7 %balls.1 = (bf16[8192,256]{1,0:T(8,128)(2,1)S(1)}, bf16[128,256]{1,0:T(8,128)(2,1)S(1)}) custom-call(s32[8192]{0:T(1024)S(1)} %broadcast_subtract_fusion.order_ref, s32[32]{0:T(128)S(1)} %copy-done.7, bf16[8192,256]{1,0:T(8,128)(2,1)} %points_ref.1, bf16[3,256,256]{2,1,0:T(8,128)(2,1)S(1)} %pad_maximum_fusion.proj_ref, bf16[256,256]{1,0:T(8,128)(2,1)S(1)} %copy-done.4, ...), custom_call_target="tpu_custom_call" | custom-call | tf_op jit(solution)/shard_map/balls/pallas_call | solution.py:133
  128.5 0.0 copy-start
  128.5 2.0 copy-done
  130.6 0.0 copy-start.1
  130.6 2.2 %copy-done.1 = bf16[8192,256]{1,0:T(8,128)(2,1)S(1)} copy-done((bf16[8192,256]{1,0:T(8,128)(2,1)S(1)}, bf16[8192,256]{1,0:T(8,128)(2,1)}, u32[]{:S(2)}) %copy-start.1) | copy-done | bytes 4194328
  132.8 72.0 %coarse.1 = (bf16[128,256]{1,0:T(8,128)(2,1)S(1)}, bf16[8192,256]{1,0:T(8,128)(2,1)S(1)}) custom-call(bf16[128,256]{1,0:T(8,128)(2,1)S(1)} %get-tuple-element.9.pooled_ref, bf16[8192,256]{1,0:T(8,128)(2,1)S(1)} %copy-done.1, bf16[3,256,256]{2,1,0:T(8,128)(2,1)S(1)} %get-tuple-element.22.cproj_ref, bf16[256,256]{1,0:T(8,128)(2,1)S(1)} %copy-done.5, ...), custom_call_target="tpu_custom_call" | custom-call | tf_op jit(solution)/shard_map/coarse/pallas_call | solution.py:251
  204.8 12.7 %unpool.1 = bf16[8192,256]{1,0:T(8,128)(2,1)} custom-call(s32[32]{0:T(128)S(1)} %copy-done.7, bf16[128,256]{1,0:T(8,128)(2,1)S(1)} %get-tuple-element.11.summary_ref, bf16[256,16384]{1,0:T(8,128)(2,1)S(1)} %bitcast.31, bf16[8192,256]{1,0:T(8,128)(2,1)S(1)} %get-tuple-element.12.refined_ref), custom_call_target="tpu_custom_call" | custom-call | tf_op jit(solution)/shard_map/unpool/pallas_call | solution.py:303
  (12 shorter events, 0.1 us)
Async XLA Ops:
  0.0 4.8 %copy-start.7 = (s32[32]{0:T(128)S(1)}, s32[32]{0:T(128)}, u32[]{:S(2)}) copy-start(s32[32]{0:T(128)} %counts_ref.3) | copy-start | bytes 388
  0.0 4.8 %copy-start.4 = (bf16[256,256]{1,0:T(8,128)(2,1)S(1)}, bf16[256,256]{1,0:T(8,128)(2,1)}, u32[]{:S(2)}) copy-start(bf16[256,256]{1,0:T(8,128)(2,1)} %out_ref.1) | copy-start | bytes 393220
  4.8 200.0 %slice-start = ((s8[8388608]{0:T(1024)(128)(4,1)}), s8[4194304]{0:T(1024)(128)(4,1)S(1)}, s32[]{:S(2)}) async-start(s8[8388608]{0:T(1024)(128)(4,1)} %bitcast.30), calls=%async_computation | async-start | bytes 8388608
  4.8 125.7 %copy-start.2 = (bf16[256,1024]{1,0:T(8,128)(2,1)S(1)}, bf16[256,1024]{1,0:T(8,128)(2,1)}, u32[]{:S(2)}) copy-start(bf16[256,1024]{1,0:T(8,128)(2,1)} %win_ref.1) | copy-start | bytes 1572868
  4.8 125.7 %copy-start.3 = (bf16[1024,256]{1,0:T(8,128)(2,1)S(1)}, bf16[1024,256]{1,0:T(8,128)(2,1)}, u32[]{:S(2)}) copy-start(bf16[1024,256]{1,0:T(8,128)(2,1)} %wout_ref.1) | copy-start | bytes 1572868
  4.8 125.7 %copy-start.5 = (bf16[256,256]{1,0:T(8,128)(2,1)S(1)}, bf16[256,256]{1,0:T(8,128)(2,1)}, u32[]{:S(2)}) copy-start(bf16[256,256]{1,0:T(8,128)(2,1)} %cout_ref.1) | copy-start | bytes 393220
  4.8 125.7 %copy-start.6 = (bf16[256,256]{1,0:T(8,128)(2,1)S(1)}, bf16[256,256]{1,0:T(8,128)(2,1)}, u32[]{:S(2)}) copy-start(bf16[256,256]{1,0:T(8,128)(2,1)} %gout_ref.1) | copy-start | bytes 393220
  4.9 199.9 %slice-start.1 = ((s8[8388608]{0:T(1024)(128)(4,1)}), s8[4194304]{0:T(1024)(128)(4,1)S(1)}, s32[]{:S(2)}) async-start(s8[8388608]{0:T(1024)(128)(4,1)} %bitcast.30), calls=%async_computation.1 | async-start | bytes 8388608
  128.5 2.0 copy-start
  130.6 2.2 %copy-start.1 = (bf16[8192,256]{1,0:T(8,128)(2,1)S(1)}, bf16[8192,256]{1,0:T(8,128)(2,1)}, u32[]{:S(2)}) copy-start(bf16[8192,256]{1,0:T(8,128)(2,1)} %copy-done) | copy-start | bytes 12582916
where the time goes:
time: 218 us; the launch traced here: 217 us
  Pallas kernels  208 us (95%)
  local copies, waits for them, and re-layouts  8.01 us (4%)
    pallas_call x1, Pallas kernels, ball_call(): pl.pallas_call(ball_kernel, grid_spec=pltpu.PrefetchScalarGridSpec(num_sc...  124 us
    pallas_call x1, Pallas kernels, coarse_call(): pl.pallas_call(functools.partial(coarse_kernel, n), in_specs=[vmem] * 8,...  72 us
    pallas_call x1, Pallas kernels, unpool_call(): pl.pallas_call(functools.partial(unpool_kernel, half), grid_spec=pltpu.Pr...  12.7 us
    unnamed x26, local copies, waits for them, and re-layouts  4.83 us

commit v1 on v0

--- a/solution.py
+++ b/solution.py
@@ -33,7 +33,7 @@
     return jnp.dot(a, b, preferred_element_type=F32)
 
 
-def attend(q_in, kv_in, proj_ref, out_weight, valid):
+def attend(q_in, kv_in, proj_ref, out_weight, count, between=None):
     feature = q_in.shape[1]
     head = feature // HEADS
     rows, keys = q_in.shape[0], kv_in.shape[0]
@@ -42,30 +42,45 @@
     k = nn(kv_in, proj_ref[1]).astype(BF16)
     v_t = nt(proj_ref[2], kv_in).astype(BF16)
     ones = jnp.ones((16, keys), BF16)
+    lane = lax.broadcasted_iota(jnp.int32, (1, feature), 1) // head
+    valid = None
+    if count is not None:
+        valid = lax.broadcasted_iota(jnp.int32, (keys, rows), 0) < count
     outs = []
-    for h in range(HEADS):
-        lo, hi = h * head, (h + 1) * head
-        parts = []
-        if lo:
-            parts.append(jnp.zeros((lo, rows), BF16))
-        parts.append(q_t[lo:hi])
-        if hi < feature:
-            parts.append(jnp.zeros((feature - hi, rows), BF16))
-        scores = nn(k, jnp.concatenate(parts, axis=0))
-        if valid is not None:
-            scores = jnp.where(valid, scores, -1e30)
-        top = jnp.max(scores, axis=0, keepdims=True)
-        expo = jnp.exp2(scores - top).astype(BF16)
-        mixed = nn(jnp.concatenate([v_t[lo:hi], ones], axis=0), expo)
-        outs.append((mixed[:head] * (1.0 / mixed[head : head + 1])).astype(BF16))
+    together = 4
+    for h0 in range(0, HEADS, together):
+        own = [k * jnp.where(lane == h, 1.0, 0.0).astype(BF16) for h in range(h0, h0 + together)]
+        all_scores = nn(jnp.concatenate(own, axis=0), q_t)
+        for h in range(h0, h0 + together):
+            lo, hi = h * head, (h + 1) * head
+            scores = all_scores[(h - h0) * keys : (h - h0 + 1) * keys]
+            if valid is not None:
+                scores = jnp.where(valid, scores, -1e30)
+            top = jnp.max(scores, axis=0, keepdims=True)
+            expo = jnp.exp2((scores - top).astype(BF16))
+            mixed = nn(jnp.concatenate([v_t[lo:hi], ones], axis=0), expo)
+            outs.append((mixed[:head] * (1.0 / mixed[head : head + 1])).astype(BF16))
+            if between is not None:
+                between(h)
     return lax.dot_general(
         jnp.concatenate(outs, axis=0), out_weight, TN, preferred_element_type=F32
     )
 
 
+def turn(proj_ref, turned_ref):
+    turned_ref[0] = proj_ref[0].T
+    turned_ref[1] = proj_ref[1]
+    turned_ref[2] = proj_ref[2].T
+
+
+def gelu(inputs):
+    inner = inputs * (0.7978845608028654 + 0.035677408136300125 * (inputs * inputs))
+    return inputs * (0.5 + 0.5 * jnp.tanh(inner))
+
+
 def ball_kernel(
     order_ref, counts_ref, points_ref, proj_ref, out_ref, pool_ref,
-    fine_ref, pooled_ref, wide, rows_ref, kept, pool_all,
+    fine_ref, pooled_ref, wide, rows_ref, kept, pool_all, turned_ref,
 ):
     step = pl.program_id(0)
     steps = pl.num_programs(0)
@@ -74,9 +89,18 @@
     pool_rows = pool_ref.shape[0]
     groups = row_count // POOL
 
+    offset = lax.axis_index("point") * row_count
+
+    def take(ball, slot, lo, hi):
+        wanted = [
+            wide[pl.ds(order_ref[ball * BALL + r] - offset, 1), :] for r in range(lo, hi)
+        ]
+        for r, row in zip(range(lo, hi), wanted):
+            rows_ref[slot, r : r + 1, :] = row
+
     @pl.when(step == 0)
     def _():
-        rows_ref[...] = jnp.zeros_like(rows_ref)
+        turn(proj_ref, turned_ref)
 
         def widen(t, carry):
             at = pl.ds(pl.multiple_of(t * BALL, BALL), BALL)
@@ -84,23 +108,23 @@
             return carry
 
         lax.fori_loop(0, row_count // BALL, widen, 0)
+        for lo in range(0, BALL, 16):
+            take(0, 0, lo, lo + 16)
 
     pool_all[pl.ds(pl.multiple_of(step * pool_rows, pool_rows), pool_rows), :] = pool_ref[...]
     count = counts_ref[step]
     first = step * BALL
-
-    def take(g, carry):
-        base = pl.multiple_of(g * 16, 16)
-        for r in range(16):
-            rows_ref[pl.ds(base + r, 1), :] = wide[pl.ds(order_ref[first + base + r], 1), :]
-        return carry
-
-    lax.fori_loop(0, (count + 15) // 16, take, 0)
-
-    x = rows_ref[...]
+    slot = step % 2
+    following = jnp.minimum(step + 1, steps - 1)
+    share = BALL // HEADS
+
+    def between(h):
+        for lo in range(h * share, (h + 1) * share, 16):
+            take(following, 1 - slot, lo, lo + 16)
+
+    x = rows_ref[slot]
     normed = normalize(x)
-    valid = lax.broadcasted_iota(jnp.int32, (BALL, BALL), 0) < count
-    fine = (x + attend(normed, normed, proj_ref, out_ref[...], valid)).astype(BF16)
+    fine = (x + attend(normed, normed, turned_ref, out_ref[...], count, between)).astype(BF16)
     fine_ref[...] = fine
     live = lax.broadcasted_iota(jnp.int32, (BALL, feature), 0) < count
     at = pl.ds(pl.multiple_of(first, BALL), BALL)
@@ -147,9 +171,10 @@
             ],
             scratch_shapes=[
                 pltpu.VMEM((row_count, feature), F32),
-                pltpu.VMEM((BALL, feature), F32),
+                pltpu.VMEM((2, BALL, feature), F32),
                 pltpu.VMEM((feature // 128, row_count, 128), F32),
                 pltpu.VMEM(pool_weight.shape, BF16),
+                pltpu.VMEM(proj.shape, BF16),
             ],
         ),
         out_shape=[
@@ -163,7 +188,7 @@
 
 def coarse_kernel(
     n, pooled_ref, fine_ref, cproj_ref, cout_ref, gproj_ref, gout_ref, win_ref, wout_ref,
-    summary_ref, refined_ref, arrived, state, send_sem, recv_sem,
+    summary_ref, refined_ref, arrived, state, cturned, gturned, send_sem, recv_sem,
 ):
     me = lax.axis_index("point")
     tokens, feature = pooled_ref.shape
@@ -177,6 +202,8 @@
         return carry
 
     lax.fori_loop(1, n, greet, 0)
+    turn(cproj_ref, cturned)
+    turn(gproj_ref, gturned)
     pl.semaphore_wait(barrier, n - 1)
 
     def copy_to(peer, slot, sender):
@@ -198,14 +225,14 @@
     tile = 256
 
     def mlp(t, carry):
-        at = pl.ds(pl.multiple_of(t * tile, tile), tile)
-        fine = fine_ref[at, :].astype(F32)
-        hidden = nn(normalize(fine), win_ref[...])
-        expanded = jax.nn.gelu(hidden, approximate=True).astype(BF16)
-        refined_ref[at, :] = (fine + nn(expanded, wout_ref[...])).astype(BF16)
-        return carry
-
-    lax.fori_loop(0, row_count // tile, mlp, 0)
+        for u in range(2):
+            at = pl.ds(pl.multiple_of((t * 2 + u) * tile, tile), tile)
+            fine = fine_ref[at, :].astype(F32)
+            hidden = nn(normalize(fine), win_ref[...]).astype(BF16)
+            refined_ref[at, :] = (fine + nn(gelu(hidden), wout_ref[...])).astype(BF16)
+        return carry
+
+    lax.fori_loop(0, row_count // (2 * tile), mlp, 0)
 
     def land(k, carry):
         sender = (me + k) % n
@@ -220,22 +247,27 @@
     apart = 1
     while apart < n:
 
-        def pair(p, carry, apart=apart):
+        def couple(p, apart=apart):
             low = (p // apart) * (2 * apart) + p % apart
             one = pl.ds(pl.multiple_of(low * tokens, tokens), tokens)
             two = pl.ds(pl.multiple_of((low + apart) * tokens, tokens), tokens)
             x = jnp.concatenate([state[one, :], state[two, :]], axis=0)
             normed = normalize(x)
-            x = x + attend(normed, normed, cproj_ref, cout_ref[...], None)
-            state[one, :] = x[:tokens]
-            state[two, :] = x[tokens:]
+            x = x + attend(normed, normed, cturned, cout_ref[...], None)
+            return one, two, x
+
+        def pairs(p, carry, couple=couple):
+            done = [couple(2 * p), couple(2 * p + 1)]
+            for one, two, x in done:
+                state[one, :] = x[:tokens]
+                state[two, :] = x[tokens:]
             return carry
 
-        lax.fori_loop(0, n // 2, pair, 0)
+        lax.fori_loop(0, n // 4, pairs, 0)
         apart *= 2
 
     x = state[mine, :]
-    mixed = attend(normalize(x), normalize(state[...]), gproj_ref, gout_ref[...], None)
+    mixed = attend(normalize(x), normalize(state[...]), gturned, gout_ref[...], None)
     summary_ref[...] = (x + mixed).astype(BF16)
 
     def sent(k, carry):
@@ -259,6 +291,8 @@
         scratch_shapes=[
             pltpu.VMEM((n, tokens, feature), BF16),
             pltpu.VMEM((n * tokens, feature), F32),
+            pltpu.VMEM(cproj.shape, BF16),
+            pltpu.VMEM(gproj.shape, BF16),
             pltpu.SemaphoreType.DMA((n,)),
             pltpu.SemaphoreType.DMA((n,)),
         ],
@@ -319,19 +353,14 @@
     )(counts, summary, weight, refined)
 
 
-def turned(proj):
-    return jnp.stack([proj[0].T, proj[1], proj[2].T])
-
-
 def local(
     points, tree_order, ball_counts, ball_proj, ball_out, pool_weight, coarse_proj, coarse_out,
     global_proj, global_out, unpool_weight, mlp_in, mlp_out,
 ):
     n = lax.axis_size("point")
-    order = tree_order - lax.axis_index("point") * points.shape[0]
-    fine, pooled = ball_call(order, ball_counts, points, turned(ball_proj), ball_out, pool_weight)
+    fine, pooled = ball_call(tree_order, ball_counts, points, ball_proj, ball_out, pool_weight)
     summary, refined = coarse_call(
-        n, pooled, fine, turned(coarse_proj), coarse_out, turned(global_proj), global_out, mlp_in, mlp_out
+        n, pooled, fine, coarse_proj, coarse_out, global_proj, global_out, mlp_in, mlp_out
     )
     return unpool_call(ball_counts, summary, unpool_weight, refined)
 

time: 218 us -> 136 us (0.62)
  Pallas kernels: 208 us -> 128 us
    pallas_call x1, Pallas kernels: 124 us -> 70.5 us  [ball_call(): pl.pallas_call(ball_kernel, grid_spec=pltpu.PrefetchScalarGridSpec(num_sc...]
    pallas_call x1, Pallas kernels: 72 us -> 45.3 us  [coarse_call(): pl.pallas_call(functools.partial(coarse_kernel, n), in_specs=[vmem] * 8,...]
    slice x3 -> x0, local copies, waits for them, and re-layouts: 3.18 us -> none  [turned(): return jnp.stack([proj[0].T, proj[1], proj[2].T])]
    unnamed x26 -> x28, local copies, waits for them, and re-layouts: 4.83 us -> 7.62 us
where the time goes in v1:
time: 136 us
  Pallas kernels  128 us (94%)
  local copies, waits for them, and re-layouts  7.62 us (6%)
    pallas_call x1, Pallas kernels, ball_call(): pl.pallas_call(ball_kernel, grid_spec=pltpu.PrefetchScalarGridSpec(num_sc...  70.5 us
    pallas_call x1, Pallas kernels, coarse_call(): pl.pallas_call(functools.partial(coarse_kernel, n), in_specs=[vmem] * 8,...  45.3 us
    pallas_call x1, Pallas kernels, unpool_call(): pl.pallas_call(functools.partial(unpool_kernel, half), grid_spec=pltpu.Pr...  12.6 us
    unnamed x28, local copies, waits for them, and re-layouts  7.62 us

profile of v1, /device:TPU:0, one launch (start us, length us, event | category | flops | bytes accessed | tf_op | source)
XLA Modules:
  0.0 136.2 jit_solution(710456121480008621)
XLA Ops:
  0.0 0.0 copy-start.4
  0.0 0.0 copy-start.3
  0.0 0.0 copy-start.5
  0.0 1.1 copy-done.5
  1.1 0.0 copy-start.8
  1.1 0.9 copy-done.8
  2.0 0.8 copy-done.11
  2.8 0.7 copy-done.12
  3.4 0.0 copy-start
  3.4 70.5 %balls.1 = (bf16[8192,256]{1,0:T(8,128)(2,1)S(1)}, bf16[128,256]{1,0:T(8,128)(2,1)S(1)}) custom-call(s32[8192]{0:T(1024)S(1)} %copy-done.11, s32[32]{0:T(128)S(1)} %copy-done.12, bf16[8192,256]{1,0:T(8,128)(2,1)} %points_ref.1, bf16[3,256,256]{2,1,0:T(8,128)(2,1)S(1)} %copy-done.5, bf16[256,256]{1,0:T(8,128)(2,1)S(1)} %copy-done.8, bf16[16384,256]{1,0:T(8,128)(2,1)} %pool_ref.1), custom_call_target="tpu_custom_call" | custom-call | tf_op jit(solution)/shard_map/balls/pallas_call | solution.py:157
  74.0 0.0 copy-start.1
  74.0 2.0 %copy-done.1 = bf16[8192,256]{1,0:T(8,128)(2,1)} copy-done((bf16[8192,256]{1,0:T(8,128)(2,1)}, bf16[8192,256]{1,0:T(8,128)(2,1)S(1)}, u32[]{:S(2)}) %copy-start.1) | copy-done | bytes 4194328
  76.0 0.0 copy-done.4
  76.0 0.0 copy-done.3
  76.0 0.0 copy-done.6
  76.0 0.0 copy-done.7
  76.0 0.0 copy-done.9
  76.0 0.0 copy-done.10
  76.0 0.0 copy-start.2
  76.1 2.2 %copy-done.2 = bf16[8192,256]{1,0:T(8,128)(2,1)S(1)} copy-done((bf16[8192,256]{1,0:T(8,128)(2,1)S(1)}, bf16[8192,256]{1,0:T(8,128)(2,1)}, u32[]{:S(2)}) %copy-start.2) | copy-done | bytes 4194328
  78.2 45.3 %coarse.1 = (bf16[128,256]{1,0:T(8,128)(2,1)S(1)}, bf16[8192,256]{1,0:T(8,128)(2,1)S(1)}) custom-call(bf16[128,256]{1,0:T(8,128)(2,1)S(1)} %get-tuple-element.9.pooled_ref, bf16[8192,256]{1,0:T(8,128)(2,1)S(1)} %copy-done.2, bf16[3,256,256]{2,1,0:T(8,128)(2,1)S(1)} %copy-done.6, bf16[256,256]{1,0:T(8,128)(2,1)S(1)} %copy-done.9, ...), custom_call_target="tpu_custom_call" | custom-call | tf_op jit(solution)/shard_map/coarse/pallas_call | solution.py:283
  123.5 0.0 copy-done
  123.6 0.0 copy-done.13
  123.6 12.6 %unpool.1 = bf16[8192,256]{1,0:T(8,128)(2,1)} custom-call(s32[32]{0:T(128)S(1)} %copy-done.13, bf16[128,256]{1,0:T(8,128)(2,1)S(1)} %get-tuple-element.11.summary_ref, bf16[256,16384]{1,0:T(8,128)(2,1)S(1)} %copy-done, bf16[8192,256]{1,0:T(8,128)(2,1)S(1)} %get-tuple-element.12.refined_ref), custom_call_target="tpu_custom_call" | custom-call | tf_op jit(solution)/shard_map/unpool/pallas_call | solution.py:337
  (7 shorter events, 0.0 us)
Async XLA Ops:
  0.0 76.0 %copy-start.4 = (bf16[1024,256]{1,0:T(8,128)(2,1)S(1)}, bf16[1024,256]{1,0:T(8,128)(2,1)}, u32[]{:S(2)}) copy-start(bf16[1024,256]{1,0:T(8,128)(2,1)} %wout_ref.1) | copy-start | bytes 1572868
  0.0 76.0 %copy-start.3 = (bf16[256,1024]{1,0:T(8,128)(2,1)S(1)}, bf16[256,1024]{1,0:T(8,128)(2,1)}, u32[]{:S(2)}) copy-start(bf16[256,1024]{1,0:T(8,128)(2,1)} %win_ref.1) | copy-start | bytes 1572868
  0.0 1.1 copy-start.5
  1.1 0.9 copy-start.8
  2.0 0.8 copy-start.11
  2.8 0.7 copy-start.12
  3.4 72.6 %copy-start.6 = (bf16[3,256,256]{2,1,0:T(8,128)(2,1)S(1)}, bf16[3,256,256]{2,1,0:T(8,128)(2,1)}, u32[]{:S(2)}) copy-start(bf16[3,256,256]{2,1,0:T(8,128)(2,1)} %cproj_ref.1) | copy-start | bytes 1179652
  3.4 72.6 %copy-start.7 = (bf16[3,256,256]{2,1,0:T(8,128)(2,1)S(1)}, bf16[3,256,256]{2,1,0:T(8,128)(2,1)}, u32[]{:S(2)}) copy-start(bf16[3,256,256]{2,1,0:T(8,128)(2,1)} %gproj_ref.1) | copy-start | bytes 1179652
  3.4 72.6 %copy-start.9 = (bf16[256,256]{1,0:T(8,128)(2,1)S(1)}, bf16[256,256]{1,0:T(8,128)(2,1)}, u32[]{:S(2)}) copy-start(bf16[256,256]{1,0:T(8,128)(2,1)} %cout_ref.1) | copy-start | bytes 393220
  3.4 72.6 %copy-start.10 = (bf16[256,256]{1,0:T(8,128)(2,1)S(1)}, bf16[256,256]{1,0:T(8,128)(2,1)}, u32[]{:S(2)}) copy-start(bf16[256,256]{1,0:T(8,128)(2,1)} %gout_ref.1) | copy-start | bytes 393220
  3.4 120.1 %copy-start = (bf16[256,16384]{1,0:T(8,128)(2,1)S(1)}, bf16[256,16384]{1,0:T(8,128)(2,1)}, u32[]{:S(2)}) copy-start(bf16[256,16384]{1,0:T(8,128)(2,1)} %weight_ref.1) | copy-start | bytes 25165828
  74.0 2.0 %copy-start.1 = (bf16[8192,256]{1,0:T(8,128)(2,1)}, bf16[8192,256]{1,0:T(8,128)(2,1)S(1)}, u32[]{:S(2)}) copy-start(bf16[8192,256]{1,0:T(8,128)(2,1)S(1)} %get-tuple-element.10.fine_ref) | copy-start | bytes 12582916
  76.0 47.6 %copy-start.13 = (s32[32]{0:T(128)S(1)}, s32[32]{0:T(128)}, u32[]{:S(2)}) copy-start(s32[32]{0:T(128)} %counts_ref.3) | copy-start | bytes 388
  76.0 2.2 %copy-start.2 = (bf16[8192,256]{1,0:T(8,128)(2,1)S(1)}, bf16[8192,256]{1,0:T(8,128)(2,1)}, u32[]{:S(2)}) copy-start(bf16[8192,256]{1,0:T(8,128)(2,1)} %copy-done.1) | copy-start | bytes 12582916

commit v2 on v1

--- a/solution.py
+++ b/solution.py
@@ -79,8 +79,8 @@
 
 
 def ball_kernel(
-    order_ref, counts_ref, points_ref, proj_ref, out_ref, pool_ref,
-    fine_ref, pooled_ref, wide, rows_ref, kept, pool_all, turned_ref,
+    order_ref, counts_ref, points_ref, proj_ref, out_ref, win_ref, wout_ref, pool_ref,
+    refined_ref, pooled_ref, wide, rows_ref, kept, pool_all, turned_ref, before,
 ):
     step = pl.program_id(0)
     steps = pl.num_programs(0)
@@ -101,6 +101,7 @@
     @pl.when(step == 0)
     def _():
         turn(proj_ref, turned_ref)
+        before[...] = jnp.zeros_like(before)
 
         def widen(t, carry):
             at = pl.ds(pl.multiple_of(t * BALL, BALL), BALL)
@@ -111,29 +112,78 @@
         for lo in range(0, BALL, 16):
             take(0, 0, lo, lo + 16)
 
-    pool_all[pl.ds(pl.multiple_of(step * pool_rows, pool_rows), pool_rows), :] = pool_ref[...]
-    count = counts_ref[step]
-    first = step * BALL
+    piece = jnp.minimum(step, steps - 2)
+    pool_all[pl.ds(pl.multiple_of(piece * pool_rows, pool_rows), pool_rows), :] = pool_ref[...]
+    last = steps - 1
+    ball = jnp.minimum(step, last - 1)
+    count = counts_ref[ball]
+    first = ball * BALL
     slot = step % 2
-    following = jnp.minimum(step + 1, steps - 1)
+    following = jnp.minimum(step + 1, last - 1)
     share = BALL // HEADS
-
-    def between(h):
-        for lo in range(h * share, (h + 1) * share, 16):
-            take(following, 1 - slot, lo, lo + 16)
-
-    x = rows_ref[slot]
-    normed = normalize(x)
-    fine = (x + attend(normed, normed, turned_ref, out_ref[...], count, between)).astype(BF16)
-    fine_ref[...] = fine
-    live = lax.broadcasted_iota(jnp.int32, (BALL, feature), 0) < count
-    at = pl.ds(pl.multiple_of(first, BALL), BALL)
-    masked = jnp.where(live, fine.astype(F32), 0.0)
-    for c in range(feature // 128):
-        kept[c, at, :] = masked[:, c * 128 : (c + 1) * 128]
-
-    @pl.when(step == steps - 1)
-    def _():
+    width = win_ref.shape[1] // 4
+
+    def mlp_parts():
+        fine = before[...]
+        normed = normalize(fine)
+        total = [fine]
+
+        def part(c):
+            columns = slice(c * width, (c + 1) * width)
+            hidden = nn(normed, win_ref[:, columns]).astype(BF16)
+            total[0] = total[0] + nn(gelu(hidden), wout_ref[columns, :])
+
+        def end():
+            refined_ref[...] = total[0].astype(BF16)
+
+        return part, end
+
+    def run(keys, rows):
+        part, end = mlp_parts()
+
+        def between(h):
+            for lo in range(h * share, (h + 1) * share, 16):
+                take(following, 1 - slot, lo, lo + 16)
+            if h % 2 == 0:
+                part(h // 2)
+
+        x = rows_ref[slot, :rows, :]
+        normed = normalize(x)
+        mixed = attend(normed, normed[:keys], turned_ref, out_ref[...], count, between)
+        end()
+        fine = (x + mixed).astype(BF16).astype(F32)
+        live = lax.broadcasted_iota(jnp.int32, (rows, feature), 0) < count
+        masked = jnp.where(live, fine, 0.0)
+        before[:rows, :] = fine
+        at = pl.ds(pl.multiple_of(first, BALL), rows)
+        for c in range(feature // 128):
+            kept[c, at, :] = masked[:, c * 128 : (c + 1) * 128]
+        if rows < BALL:
+            before[rows:, :] = jnp.zeros((BALL - rows, feature), F32)
+            rest = pl.ds(pl.multiple_of(first + rows, 128), BALL - rows)
+            for c in range(feature // 128):
+                kept[c, rest, :] = jnp.zeros((BALL - rows, 128), F32)
+
+    balls_left = step < last
+
+    @pl.when(jnp.logical_and(balls_left, count <= 128))
+    def _():
+        run(128, 128)
+
+    @pl.when(jnp.logical_and(balls_left, jnp.logical_and(count > 128, count <= 192)))
+    def _():
+        run(192, BALL)
+
+    @pl.when(jnp.logical_and(balls_left, count > 192))
+    def _():
+        run(BALL, BALL)
+
+    @pl.when(step == last)
+    def _():
+        part, end = mlp_parts()
+        for c in range(4):
+            part(c)
+        end()
         per = 8
 
         def pool(c, total):
@@ -148,7 +198,7 @@
         pooled_ref[...] = total.astype(BF16)
 
 
-def ball_call(order, counts, points, proj, out_weight, pool_weight):
+def ball_call(order, counts, points, proj, out_weight, mlp_in, mlp_out, pool_weight):
     row_count, feature = points.shape
     steps = row_count // BALL
     groups = row_count // POOL
@@ -158,15 +208,17 @@
         ball_kernel,
         grid_spec=pltpu.PrefetchScalarGridSpec(
             num_scalar_prefetch=2,
-            grid=(steps,),
+            grid=(steps + 1,),
             in_specs=[
                 pl.BlockSpec((row_count, feature), lambda i, *_: (0, 0), pipeline_mode=once),
                 pl.BlockSpec(proj.shape, lambda i, *_: (0, 0, 0), pipeline_mode=once),
                 pl.BlockSpec(out_weight.shape, lambda i, *_: (0, 0), pipeline_mode=once),
-                pl.BlockSpec((pool_rows, feature), lambda i, *_: (i, 0)),
+                pl.BlockSpec(mlp_in.shape, lambda i, *_: (0, 0), pipeline_mode=once),
+                pl.BlockSpec(mlp_out.shape, lambda i, *_: (0, 0), pipeline_mode=once),
+                pl.BlockSpec((pool_rows, feature), lambda i, *_: (jnp.minimum(i, steps - 1), 0)),
             ],
             out_specs=[
-                pl.BlockSpec((BALL, feature), lambda i, *_: (i, 0)),
+                pl.BlockSpec((BALL, feature), lambda i, *_: (jnp.maximum(i - 1, 0), 0)),
                 pl.BlockSpec((groups, feature), lambda i, *_: (0, 0)),
             ],
             scratch_shapes=[
@@ -175,24 +227,23 @@
                 pltpu.VMEM((feature // 128, row_count, 128), F32),
                 pltpu.VMEM(pool_weight.shape, BF16),
                 pltpu.VMEM(proj.shape, BF16),
+                pltpu.VMEM((BALL, feature), F32),
             ],
         ),
         out_shape=[
             jax.ShapeDtypeStruct((row_count, feature), BF16),
             jax.ShapeDtypeStruct((groups, feature), BF16),
         ],
-        compiler_params=pltpu.CompilerParams(vmem_limit_bytes=48 * 1024 * 1024),
+        compiler_params=pltpu.CompilerParams(vmem_limit_bytes=58 * 1024 * 1024),
         name="balls",
-    )(order, counts, points, proj, out_weight, pool_weight)
+    )(order, counts, points, proj, out_weight, mlp_in, mlp_out, pool_weight)
 
 
 def coarse_kernel(
-    n, pooled_ref, fine_ref, cproj_ref, cout_ref, gproj_ref, gout_ref, win_ref, wout_ref,
-    summary_ref, refined_ref, arrived, state, cturned, gturned, send_sem, recv_sem,
+    n, pooled_ref, cproj_ref, cout_ref, gproj_ref, gout_ref, summary_ref, arrived, state, cturned, gturned, send_sem, recv_sem,
 ):
     me = lax.axis_index("point")
     tokens, feature = pooled_ref.shape
-    row_count = fine_ref.shape[0]
 
     barrier = pltpu.get_barrier_semaphore()
 
@@ -202,8 +253,6 @@
         return carry
 
     lax.fori_loop(1, n, greet, 0)
-    turn(cproj_ref, cturned)
-    turn(gproj_ref, gturned)
     pl.semaphore_wait(barrier, n - 1)
 
     def copy_to(peer, slot, sender):
@@ -221,18 +270,8 @@
         return carry
 
     lax.fori_loop(1, n, send, 0)
-
-    tile = 256
-
-    def mlp(t, carry):
-        for u in range(2):
-            at = pl.ds(pl.multiple_of((t * 2 + u) * tile, tile), tile)
-            fine = fine_ref[at, :].astype(F32)
-            hidden = nn(normalize(fine), win_ref[...]).astype(BF16)
-            refined_ref[at, :] = (fine + nn(gelu(hidden), wout_ref[...])).astype(BF16)
-        return carry
-
-    lax.fori_loop(0, row_count // (2 * tile), mlp, 0)
+    turn(cproj_ref, cturned)
+    turn(gproj_ref, gturned)
 
     def land(k, carry):
         sender = (me + k) % n
@@ -277,17 +316,14 @@
     lax.fori_loop(1, n, sent, 0)
 
 
-def coarse_call(n, pooled, fine, cproj, cout, gproj, gout, mlp_in, mlp_out):
+def coarse_call(n, pooled, cproj, cout, gproj, gout):
     tokens, feature = pooled.shape
     vmem = pl.BlockSpec(memory_space=pltpu.VMEM)
     return pl.pallas_call(
         functools.partial(coarse_kernel, n),
-        in_specs=[vmem] * 8,
-        out_specs=[vmem] * 2,
-        out_shape=[
-            jax.ShapeDtypeStruct((tokens, feature), BF16),
-            jax.ShapeDtypeStruct(fine.shape, BF16),
-        ],
+        in_specs=[vmem] * 5,
+        out_specs=vmem,
+        out_shape=jax.ShapeDtypeStruct((tokens, feature), BF16),
         scratch_shapes=[
             pltpu.VMEM((n, tokens, feature), BF16),
             pltpu.VMEM((n * tokens, feature), F32),
@@ -297,10 +333,10 @@
             pltpu.SemaphoreType.DMA((n,)),
         ],
         compiler_params=pltpu.CompilerParams(
-            collective_id=0, has_side_effects=True, vmem_limit_bytes=40 * 1024 * 1024
+            collective_id=0, has_side_effects=True, vmem_limit_bytes=32 * 1024 * 1024
         ),
         name="coarse",
-    )(pooled, fine, cproj, cout, gproj, gout, mlp_in, mlp_out)
+    )(pooled, cproj, cout, gproj, gout)
 
 
 def unpool_kernel(half, counts_ref, summary_ref, weight_ref, refined_ref, out_ref, spread):
@@ -348,7 +384,7 @@
             scratch_shapes=[pltpu.VMEM((feature // 128, row_count, 128), F32)],
         ),
         out_shape=jax.ShapeDtypeStruct((row_count, feature), BF16),
-        compiler_params=pltpu.CompilerParams(vmem_limit_bytes=32 * 1024 * 1024),
+        compiler_params=pltpu.CompilerParams(vmem_limit_bytes=24 * 1024 * 1024),
         name="unpool",
     )(counts, summary, weight, refined)
 
@@ -358,10 +394,10 @@
     global_proj, global_out, unpool_weight, mlp_in, mlp_out,
 ):
     n = lax.axis_size("point")
-    fine, pooled = ball_call(tree_order, ball_counts, points, ball_proj, ball_out, pool_weight)
-    summary, refined = coarse_call(
-        n, pooled, fine, coarse_proj, coarse_out, global_proj, global_out, mlp_in, mlp_out
+    refined, pooled = ball_call(
+        tree_order, ball_counts, points, ball_proj, ball_out, mlp_in, mlp_out, pool_weight
     )
+    summary = coarse_call(n, pooled, coarse_proj, coarse_out, global_proj, global_out)
     return unpool_call(ball_counts, summary, unpool_weight, refined)
 
 

time: 136 us -> 133 us (0.978); the launches traced: 136 us -> 131 us
  Pallas kernels: 128 us -> 125 us
    pallas_call x1, Pallas kernels: 45.3 us -> 37.5 us  [coarse_call(): pl.pallas_call(functools.partial(coarse_kernel, n), in_specs=[vmem] * 5,...]
    pallas_call x1, Pallas kernels: 70.5 us -> 74.6 us  [ball_call(): pl.pallas_call(ball_kernel, grid_spec=pltpu.PrefetchScalarGridSpec(num_sc...]
    unnamed x28 -> x16, local copies, waits for them, and re-layouts: 7.62 us -> 6.42 us
where the time goes in v2:
time: 133 us; the launch traced here: 131 us
  Pallas kernels  125 us (94%)
  local copies, waits for them, and re-layouts  6.42 us (5%)
    pallas_call x1, Pallas kernels, ball_call(): pl.pallas_call(ball_kernel, grid_spec=pltpu.PrefetchScalarGridSpec(num_sc...  74.6 us
    pallas_call x1, Pallas kernels, coarse_call(): pl.pallas_call(functools.partial(coarse_kernel, n), in_specs=[vmem] * 5,...  37.5 us
    pallas_call x1, Pallas kernels, unpool_call(): pl.pallas_call(functools.partial(unpool_kernel, half), grid_spec=pltpu.Pr...  12.7 us
    unnamed x16, local copies, waits for them, and re-layouts  6.42 us

profile of v2, /device:TPU:0, one launch (start us, length us, event | category | flops | bytes accessed | tf_op | source)
XLA Modules:
  0.0 131.3 jit_solution(17935489812679620498)
XLA Ops:
  0.0 0.0 copy-start.7
  0.0 0.0 copy-start.5
  0.0 0.0 copy-start.3
  0.0 0.0 copy-start.4
  0.0 0.0 copy-start.2
  0.0 74.6 %balls.1 = (bf16[8192,256]{1,0:T(8,128)(2,1)}, bf16[128,256]{1,0:T(8,128)(2,1)}) custom-call(s32[8192]{0:T(1024)} %order_ref.1, s32[32]{0:T(128)} %counts_ref.3, bf16[8192,256]{1,0:T(8,128)(2,1)} %points_ref.1, bf16[3,256,256]{2,1,0:T(8,128)(2,1)} %proj_ref.1, bf16[256,256]{1,0:T(8,128)(2,1)} %out_ref.1, bf16[256,1024]{1,0:T(8,128)(2,1)} %win_ref.1, ...), custom_call_target="tpu_custom_call" | custom-call | tf_op jit(solution)/shard_map/balls/pallas_call | solution.py:207
  74.6 0.0 copy-done.5
  74.6 0.0 copy-done.3
  74.7 0.0 copy-done.4
  74.7 0.0 copy-done.2
  74.7 0.0 copy-start.6
  74.7 0.8 copy-done.6
  75.5 37.5 %coarse.1.summary_ref = bf16[128,256]{1,0:T(8,128)(2,1)S(1)} custom-call(bf16[128,256]{1,0:T(8,128)(2,1)S(1)} %copy-done.6, bf16[3,256,256]{2,1,0:T(8,128)(2,1)S(1)} %copy-done.2, bf16[256,256]{1,0:T(8,128)(2,1)S(1)} %copy-done.4, bf16[3,256,256]{2,1,0:T(8,128)(2,1)S(1)} %copy-done.3, bf16[256,256]{1,0:T(8,128)(2,1)S(1)} %copy-done.5), custom_call_target="tpu_custom_call" | custom-call | tf_op jit(solution)/shard_map/coarse/pallas_call | solution.py:322
  113.0 0.0 copy-done.7
  113.0 0.0 copy-start
  113.0 3.4 %copy-done = bf16[256,16384]{1,0:T(8,128)(2,1)S(1)} copy-done((bf16[256,16384]{1,0:T(8,128)(2,1)S(1)}, bf16[256,16384]{1,0:T(8,128)(2,1)}, u32[]{:S(2)}) %copy-start) | copy-done | bytes 8388632
  116.4 0.0 copy-start.1
  116.4 2.2 %copy-done.1 = bf16[8192,256]{1,0:T(8,128)(2,1)S(1)} copy-done((bf16[8192,256]{1,0:T(8,128)(2,1)S(1)}, bf16[8192,256]{1,0:T(8,128)(2,1)}, u32[]{:S(2)}) %copy-start.1) | copy-done | bytes 4194328
  118.6 12.7 %unpool.1 = bf16[8192,256]{1,0:T(8,128)(2,1)} custom-call(s32[32]{0:T(128)S(1)} %copy-done.7, bf16[128,256]{1,0:T(8,128)(2,1)S(1)} %coarse.1.summary_ref, bf16[256,16384]{1,0:T(8,128)(2,1)S(1)} %copy-done, bf16[8192,256]{1,0:T(8,128)(2,1)S(1)} %copy-done.1), custom_call_target="tpu_custom_call" | custom-call | tf_op jit(solution)/shard_map/unpool/pallas_call | solution.py:373
Async XLA Ops:
  0.0 113.0 %copy-start.7 = (s32[32]{0:T(128)S(1)}, s32[32]{0:T(128)}, u32[]{:S(2)}) copy-start(s32[32]{0:T(128)} %counts_ref.3) | copy-start | bytes 388
  0.0 74.6 %copy-start.5 = (bf16[256,256]{1,0:T(8,128)(2,1)S(1)}, bf16[256,256]{1,0:T(8,128)(2,1)}, u32[]{:S(2)}) copy-start(bf16[256,256]{1,0:T(8,128)(2,1)} %gout_ref.1) | copy-start | bytes 393220
  0.0 74.6 %copy-start.3 = (bf16[3,256,256]{2,1,0:T(8,128)(2,1)S(1)}, bf16[3,256,256]{2,1,0:T(8,128)(2,1)}, u32[]{:S(2)}) copy-start(bf16[3,256,256]{2,1,0:T(8,128)(2,1)} %gproj_ref.1) | copy-start | bytes 1179652
  0.0 74.7 %copy-start.4 = (bf16[256,256]{1,0:T(8,128)(2,1)S(1)}, bf16[256,256]{1,0:T(8,128)(2,1)}, u32[]{:S(2)}) copy-start(bf16[256,256]{1,0:T(8,128)(2,1)} %cout_ref.1) | copy-start | bytes 393220
  0.0 74.7 %copy-start.2 = (bf16[3,256,256]{2,1,0:T(8,128)(2,1)S(1)}, bf16[3,256,256]{2,1,0:T(8,128)(2,1)}, u32[]{:S(2)}) copy-start(bf16[3,256,256]{2,1,0:T(8,128)(2,1)} %cproj_ref.1) | copy-start | bytes 1179652
  74.7 0.8 copy-start.6
  113.0 3.4 %copy-start = (bf16[256,16384]{1,0:T(8,128)(2,1)S(1)}, bf16[256,16384]{1,0:T(8,128)(2,1)}, u32[]{:S(2)}) copy-start(bf16[256,16384]{1,0:T(8,128)(2,1)} %weight_ref.1) | copy-start | bytes 25165828
  116.4 2.2 %copy-start.1 = (bf16[8192,256]{1,0:T(8,128)(2,1)S(1)}, bf16[8192,256]{1,0:T(8,128)(2,1)}, u32[]{:S(2)}) copy-start(bf16[8192,256]{1,0:T(8,128)(2,1)} %get-tuple-element.8.refined_ref) | copy-start | bytes 12582916
